TPU v7x, 256 devices: a whole 4x4x8 slice. The times are simulated.
256 devices in a mesh: ctx: 64 (over x, z, core), head: 4 (over y).
Axes of the slice: x: 4, y: 4, z: 8, core: 2. Of those that a mesh axis runs over, the one named last changes fastest.
Arguments:
- conv_in: bfloat16 [32768, 2048], P('ctx', 'head'), may hold values from -6 to 6
- conv_weight: float32 [4, 2048], P(None, 'head'), may hold values from -3 to 3
- conv_bias: float32 [2048], P('head'), may hold values from -3 to 3
- qk_weight: bfloat16 [2, 8, 256, 256], P(None, 'head'), may hold values from -0.375 to 0.375
- value_in: bfloat16 [32768, 4096], P('ctx', 'head'), may hold values from -6 to 6
- gate_pre: float32 [2, 8, 32768], P(None, 'head', 'ctx'), may hold values from -6 to 300, as said below
- norm_gain: float32 [4096], P('head'), may hold values from 0.5 to 1.5
- out_weight: bfloat16 [4096, 4096], P('head'), may hold values from -0.125 to 0.125
Outputs:
- layer_out: bfloat16 [32768, 4096], P('ctx', 'head')
Inputs may be any that keep to these rules, and one draw needn't show every extreme that they name: gate_pre[0] holds input-gate preactivations and gate_pre[1] forget-gate preactivations.
All inputs are finite; a program needn't handle non-finite values.
Results may differ from a plain program's by a relative error of at most 0.02.
Values may be sent and summed in bfloat16 or wider, within the bound.
A program may use at most 192 MiB of HBM per device.

v0:
```python
import jax
import jax.numpy as jnp
from jax import lax
from jax.sharding import PartitionSpec as P

BLOCK = 512


def from_behind(block, axis, distance):
    devices = range(lax.axis_size(axis))
    route = [(i - distance, i) for i in devices if i - distance in devices]
    return lax.ppermute(block, axis, route)


def prefix(part, axis, combine, identity):
    place = lax.axis_index(axis)
    gathered = jax.tree.map(lambda a: lax.all_gather(a, axis), part)
    state = jax.tree.map(lambda a, e: jnp.zeros_like(a) + jnp.asarray(e, a.dtype), part, identity)

    def one(lap, state):
        return combine(
            state, jax.tree.map(lambda a: lax.dynamic_index_in_dim(a, lap, 0, False), gathered)
        )

    return lax.fori_loop(0, place, one, state)


def local_block(carry_state, block_data):
    state_mat, state_max, decay_base = carry_state
    queries, key_rows, values, in_gate, log_forget = block_data
    block_len = in_gate.shape[1]
    cum_decay = jnp.cumsum(log_forget, axis=1)
    row_ids = lax.broadcasted_iota(jnp.int32, (block_len, block_len), 0)
    col_ids = lax.broadcasted_iota(jnp.int32, (block_len, block_len), 1)
    log_weight = jnp.where(
        (row_ids >= col_ids)[None],
        cum_decay[:, :, None] - cum_decay[:, None, :] + in_gate[:, None, :],
        -jnp.inf,
    )
    carry_log = cum_decay + state_max[:, None]
    stabilizer = jnp.maximum(jnp.max(log_weight, axis=2), carry_log)
    scores = jnp.einsum("thd,shd->hts", queries, key_rows, preferred_element_type=jnp.float32)
    weights = (scores * jnp.exp(log_weight - stabilizer[:, :, None])).astype(jnp.bfloat16)
    inner_sum = jnp.einsum("hts,shv->thv", weights, values, preferred_element_type=jnp.float32)
    carried = jnp.einsum(
        "thd,hdv->thv", queries.astype(jnp.float32), state_mat, precision=lax.Precision.HIGHEST
    )
    numerator = inner_sum + jnp.exp(carry_log - stabilizer).T[:, :, None] * carried
    block_decay = cum_decay[:, -1]
    end_log = block_decay[:, None] - cum_decay + in_gate
    new_max = jnp.maximum(state_max + block_decay, jnp.max(end_log, axis=1))
    scaled = (
        key_rows.astype(jnp.float32) * jnp.exp(end_log - new_max[:, None]).T[:, :, None]
    ).astype(jnp.bfloat16)
    update = jnp.einsum("shd,shv->hdv", scaled, values, preferred_element_type=jnp.float32)
    state_mat = jnp.exp(state_max + block_decay - new_max)[:, None, None] * state_mat + update
    outputs = (numerator, stabilizer.T, (cum_decay + decay_base[:, None]).T)
    return ((state_mat, new_max, decay_base + block_decay), outputs)


def join_carry(earlier, later):
    mat_early, max_early, sum_early = earlier
    mat_late, max_late, sum_late = later
    joint = jnp.maximum(max_early + sum_late, max_late)
    merged = (
        jnp.exp(max_early + sum_late - joint)[:, None, None] * mat_early
        + jnp.exp(max_late - joint)[:, None, None] * mat_late
    )
    return (merged, joint, sum_early + sum_late)


def body(conv_in, conv_weight, conv_bias, qk_weight, value_in, gate_pre, norm_gain, out_weight):
    tok_rows = conv_in.shape[0]
    head_count = qk_weight.shape[1]
    key_dim = qk_weight.shape[2]
    value_dim = value_in.shape[1] // head_count
    conv_len = conv_weight.shape[0]
    rim_rows = from_behind(conv_in[tok_rows - (conv_len - 1) :], "ctx", 1)
    padded = jnp.concatenate([rim_rows, conv_in], axis=0).astype(jnp.float32)
    conv_pre = conv_bias + conv_weight[0] * padded[0:tok_rows]
    for offset in range(1, conv_len):
        conv_pre = conv_pre + conv_weight[offset] * padded[offset : offset + tok_rows]
    activated = jax.nn.silu(conv_pre).astype(jnp.bfloat16).reshape(tok_rows, head_count, key_dim)
    queries = jnp.einsum(
        "thd,hde->the", activated, qk_weight[0], preferred_element_type=jnp.float32
    ).astype(jnp.bfloat16)
    key_rows = (
        jnp.einsum("thd,hde->the", activated, qk_weight[1], preferred_element_type=jnp.float32)
        * key_dim ** (-0.5)
    ).astype(jnp.bfloat16)
    values = value_in.reshape(tok_rows, head_count, value_dim)
    in_gate = gate_pre[0]
    log_forget = jax.nn.log_sigmoid(gate_pre[1])
    num_blocks = tok_rows // BLOCK
    inputs = (
        queries.reshape(num_blocks, BLOCK, head_count, key_dim),
        key_rows.reshape(num_blocks, BLOCK, head_count, key_dim),
        values.reshape(num_blocks, BLOCK, head_count, value_dim),
        in_gate.reshape(head_count, num_blocks, BLOCK).transpose(1, 0, 2),
        log_forget.reshape(head_count, num_blocks, BLOCK).transpose(1, 0, 2),
    )
    start = (
        jnp.zeros((head_count, key_dim, value_dim), jnp.float32),
        jnp.full((head_count,), -1e30, jnp.float32),
        jnp.zeros((head_count,), jnp.float32),
    )
    summary, outputs = lax.scan(local_block, start, inputs)
    numerator = outputs[0].reshape(tok_rows, head_count, value_dim)
    local_max = outputs[1].reshape(tok_rows, head_count)
    decay_sum = outputs[2].reshape(tok_rows, head_count)
    summary_mat, summary_max, summary_decay = summary
    identity = (
        jnp.zeros_like(summary_mat),
        jnp.full_like(summary_max, -1e30),
        jnp.zeros_like(summary_decay),
    )
    carry_mat, carry_max, carry_sum = prefix(
        (summary_mat, summary_max, summary_decay), "ctx", join_carry, identity
    )
    new_max = jnp.maximum(local_max, carry_max[None, :] + decay_sum)
    carried = jnp.einsum(
        "thd,hdv->thv", queries.astype(jnp.float32), carry_mat, precision=lax.Precision.HIGHEST
    )
    numerator = (
        numerator * jnp.exp(local_max - new_max)[:, :, None]
        + jnp.exp(carry_max[None, :] + decay_sum - new_max)[:, :, None] * carried
    )
    scale_inv = lax.rsqrt(jnp.mean(numerator * numerator, axis=2, keepdims=True) + 1e-06)
    normed = (
        (numerator * scale_inv * norm_gain.reshape(head_count, value_dim))
        .astype(jnp.bfloat16)
        .reshape(tok_rows, head_count * value_dim)
    )
    partial_value = jnp.dot(normed, out_weight, preferred_element_type=jnp.float32)
    return lax.psum_scatter(
        partial_value.astype(jnp.bfloat16), "head", scatter_dimension=1, tiled=True
    )


def solution(mesh):
    return jax.shard_map(
        body,
        mesh=mesh,
        in_specs=(
            P("ctx", "head"),
            P(None, "head"),
            P("head"),
            P(None, "head", None, None),
            P("ctx", "head"),
            P(None, "head", "ctx"),
            P("head"),
            P("head", None),
        ),
        out_specs=P("ctx", "head"),
        check_vma=False,
    )
```

profile of v0, /device:TPU:1, one launch (start us, length us, event | category | flops | bytes accessed | tf_op | source)
XLA Modules:
  0.0 439.7 jit_solution(18120846343908282644)
XLA Ops:
  6.5 0.7 slice.50
  7.3 4.9 %collective-permute-start = (bf16[3,512]{1,0:T(4,128)(2,1)S(1)}, bf16[3,512]{1,0:T(4,128)(2,1)S(1)}, u32[]{:S(2)}, u32[]{:S(2)}) collective-permute-start(bf16[3,512]{1,0:T(4,128)(2,1)S(1)} %slice.50), channel_id=1, source_target_pairs={{0,4},{4,8},{8,12},{12,16},{16,20},{20,24},{24,28},{28,32},{32,36}... | collective-permute-start | bytes 9224 | tf_op jit(solution)/shard_map/ppermute | solution.py:12
  12.3 0.7 slice_negate_fusion
  13.0 0.6 reduce-window.6
  14.2 0.7 fusion.8
  14.9 0.9 exponential_bitcast_fusion.1
  15.8 0.9 fusion.49
  16.7 1.3 dynamic-slice.3
  18.8 1.2 maximum_convert_fusion
  20.0 0.7 multiply_convert_fusion.3
  20.7 0.3 copy-done.4
  21.0 0.3 fusion.11
  21.4 1.6 convolution_add_fusion
  23.1 127.2 %all-reduce = f32[128]{0:T(128)S(1)} all-reduce(f32[128]{0:T(128)S(1)} %get-tuple-element.154), channel_id=2, replica_groups=mesh['ctx'=64,'head'=4] {'ctx'}, use_global_device_ids=true, to_apply=%add | all-reduce | flops 128 | bytes 1024
  150.4 39.6 %all-gather.2 = f32[64,1,2]{2,1,0:T(1,128)S(1)} all-gather(f32[1,1,2]{2,1,0:T(1,128)S(1)} %fusion.43), channel_id=1, replica_groups=mesh['ctx'=64,'head'=4] {'ctx'}, dimensions={0}, use_global_device_ids=true | all-gather | bytes 520 | tf_op jit(solution)/shard_map/all_gather | solution.py:17
  190.4 1.0 fusion.30
  191.4 0.3 copy-done.6
  191.7 4.0 fusion.10
  195.7 66.6 %all-gather.5.cloned.1.call-done = f32[128,256,512]{2,1,0:T(8,128)} async-done(((f32[2,256,512]{2,1,0:T(8,128)}), f32[128,256,512]{2,1,0:T(8,128)}) %all-gather.5.cloned.1.call-update) | async-done | bytes 67108880 | tf_op jit(solution)/shard_map/all_gather | solution.py:17
  262.5 1.8 while.3
  262.5 1.7 fusion.58
  264.4 3.9 multiply_reduce_fusion
  268.6 9.5 %convolution_convert_fusion = bf16[512,4096]{1,0:T(8,128)(2,1)} fusion(bf16[512,1024]{0,1:T(8,128)(2,1)S(1)} %bitcast.132, bf16[1024,4096]{1,0:T(8,128)(2,1)} %param.17), kind=kOutput, calls=%fused_computation.10 | convolution fusion | flops 4297064448 | bytes 13631488 | tf_op jit(solution)/shard_map/dot_general | solution.py:134
  278.1 154.7 %reduce-scatter.2.cloned.1.call-done = bf16[512,1024]{1,0:T(8,128)(2,1)} async-done(((bf16[512,4096]{1,0:T(8,128)(2,1)}), bf16[512,1024]{1,0:T(8,128)(2,1)}) %reduce-scatter.2.cloned.1.call-update) | async-done | bytes 1048592 | tf_op jit(solution)/shard_map/reduce_scatter | solution.py:135
  (41 shorter events, 2.0 us)
Async XLA Ops:
  6.5 13.4 %copy-start.2 = (f32[512]{0:T(512)S(1)}, f32[512]{0:T(512)}, u32[]{:S(2)}) copy-start(f32[512]{0:T(512)} %param.12) | copy-start | bytes 6148
  6.5 255.8 %all-gather.5.cloned.1.call-start = ((), (), s32[]{:S(2)}) async-start(), calls=%async_computation.2 | async-start | bytes 68157440 | tf_op jit(solution)/shard_map/all_gather | solution.py:17
  7.3 11.5 %collective-permute-start = (bf16[3,512]{1,0:T(4,128)(2,1)S(1)}, bf16[3,512]{1,0:T(4,128)(2,1)S(1)}, u32[]{:S(2)}, u32[]{:S(2)}) collective-permute-start(bf16[3,512]{1,0:T(4,128)(2,1)S(1)} %slice.50), channel_id=1, source_target_pairs={{0,4},{4,8},{8,12},{12,16},{16,20},{20,24},{24,28},{28,32},{32,36}... | collective-permute-start | bytes 9224 | tf_op jit(solution)/shard_map/ppermute | solution.py:12
  20.0 1.0 copy-start.4
  20.0 1.4 copy-start.3
  21.3 168.8 %copy-start.5 = (bf16[512,2,256]{2,0,1:T(8,128)(2,1)}, bf16[512,2,256]{2,0,1:T(8,128)(2,1)S(1)}, u32[]{:S(2)}) copy-start(bf16[512,2,256]{2,0,1:T(8,128)(2,1)S(1)} %fusion.11) | copy-start | bytes 1572868
  21.3 129.1 %copy-start.1 = (f32[1024]{0:T(1024)S(1)}, f32[1024]{0:T(1024)}, u32[]{:S(2)}) copy-start(f32[1024]{0:T(1024)} %param.16) | copy-start | bytes 12292
  23.0 409.8 %reduce-scatter.2.cloned.1.call-start = ((), (), s32[]{:S(2)}) async-start(), calls=%async_computation.1 | async-start | bytes 5242880 | tf_op jit(solution)/shard_map/reduce_scatter | solution.py:135
  190.4 5.3 %copy-start = (bf16[512,2,256]{2,0,1:T(8,128)(2,1)}, bf16[512,2,256]{2,0,1:T(8,128)(2,1)S(1)}, u32[]{:S(2)}) copy-start(bf16[512,2,256]{2,0,1:T(8,128)(2,1)S(1)} %fusion.12) | copy-start | bytes 1572868
  190.4 1.3 copy-start.6
Sparse Core Ops, SparseCore 0:
  23.2 239.1 all-gather.4
  278.2 154.5 reduce-scatter.1
where the time goes:
time: 443 us; the launch traced here: 440 us
  waiting for transfers between devices  221 us (50%)
  blocking collectives  167 us (38%)
  matrix products  20.7 us (5%)
  between operations  14.3 us (3%)
  other arithmetic  7.42 us (2%)
  starting transfers between devices  4.97 us (1%)
    reduce_scatter x1, waiting for transfers between devices, body(): lax.psum_scatter(partial_value.astype(jnp.bfloat16), 'head', scatter_dime...  155 us
    unnamed x1, blocking collectives  127 us
    all_gather x1, waiting for transfers between devices, prefix(): gathered = jax.tree.map(lambda a: lax.all_gather(a, axis), part)  66.6 us
    all_gather x1, blocking collectives, prefix(): gathered = jax.tree.map(lambda a: lax.all_gather(a, axis), part)  39.6 us
    dot_general x1, matrix products, body(): jnp.dot(normed, out_weight, preferred_element_type=jnp.float32)  9.48 us
  transfers between devices with their start and end apart: 3, of which 2 were waited for; matrix products, arithmetic and copies ran while one was open for 3% of the time, Pallas kernels for 0%

commit v1 on v0

v1 whole, which is shorter than its diff:
```python
import functools

import jax
import jax.numpy as jnp
from jax import lax
from jax.experimental import pallas as pl
from jax.experimental.pallas import tpu as pltpu
from jax.sharding import PartitionSpec as P

MESH = pl.DeviceIdType.MESH
F32 = jnp.float32
BF16 = jnp.bfloat16
LOW = -1e30

T = 512
HALF = 256
DK = 256
DV = 512
DM = 4096
NY = 4
COLS = DM // NY
PIECE = 256
PIECES = COLS // PIECE


def dot(a, b):
    return jnp.dot(a, b, preferred_element_type=F32)


def scan_lanes(v, combine, fill):
    lane = lax.broadcasted_iota(jnp.int32, v.shape, 1)
    shift = 1
    while shift < v.shape[1]:
        moved = pltpu.roll(v, shift, 1)
        v = combine(v, jnp.where(lane >= shift, moved, fill))
        shift *= 2
    return v


def join(early, late):
    return jnp.maximum(early[0] + late[1], late[0]), early[1] + late[1]


def body_kernel(
    nx, nz,
    conv_hbm, cw_hbm, cb_hbm, qk_hbm, val_hbm, gate_hbm, gain_hbm, w_hbm,
    out_hbm,
    conv_v, cw, cb, qk, val, gate, gain, w, xpad, halo, act, q, kt, state, local,
    sc_own, sc_other, sc_chip, sc_row, st_send, st_recv, t_send, t_in, r_send, r_in,
    c_send, c_in, p_send, carry, normed, acc,
    two_s, two_r, dir_s, dir_r, rel_s, rel_r, out_v,
    ld_sem, halo_sem, sc_sem, scz_sem, scx_sem, st_sem, tz_sem, rx_sem, cz_sem, p_sem,
    two_sem, dir_sem, rel_sem, out_sem,
):
    n_ctx = nx * nz * 2
    slice_rows = DK // nz
    me = lax.axis_index("ctx")
    y = lax.axis_index("head")
    core = lax.rem(me, 2)
    chip = lax.div(me, 2)
    z = lax.rem(chip, nz)
    x = lax.div(chip, nz)
    other = me + 1 - 2 * core

    def z_peer(k):
        return (x * nz + lax.rem(z + k, nz)) * 2 + core

    def x_peer(k):
        return (lax.rem(x + k, nx) * nz + z) * 2 + core

    def y_peer(k):
        return lax.rem(y + k, NY)

    def remote(src, dst, sems, to, at_y=None):
        return pltpu.make_async_remote_copy(
            src_ref=src, dst_ref=dst, send_sem=sems[0], recv_sem=sems[1],
            device_id=(to, y if at_y is None else at_y), device_id_type=MESH,
        )

    loads = [
        pltpu.make_async_copy(src, dst, ld_sem.at[i])
        for i, (src, dst) in enumerate(
            [(gate_hbm, gate), (conv_hbm, conv_v), (cw_hbm, cw), (cb_hbm, cb),
             (qk_hbm, qk), (val_hbm, val), (gain_hbm, gain), (w_hbm, w)]
        )
    ]
    for load in loads:
        load.start()

    barrier = pltpu.get_barrier_semaphore()
    after = lax.rem(me + 1, n_ctx)
    before = lax.rem(me + n_ctx - 1, n_ctx)
    greet = [(after, y), (before, y), (other, y)]
    greet += [(z_peer(k), y) for k in range(1, nz)]
    greet += [(x_peer(k), y) for k in range(1, nx)]
    greet += [(me, y_peer(k)) for k in (1, 3)]
    for to in greet:
        pl.semaphore_signal(barrier, inc=1, device_id=to, device_id_type=MESH)

    loads[0].wait()
    pad = jnp.zeros((6, T), F32)
    in_gate = jnp.concatenate([gate[0], pad], axis=0)
    forget = jnp.concatenate([gate[1], pad], axis=0)
    log_forget = jnp.minimum(forget, 0.0) - jnp.log1p(jnp.exp(-jnp.abs(forget)))
    cum = scan_lanes(log_forget, jnp.add, 0.0)
    g = in_gate - cum
    cm = scan_lanes(g, jnp.maximum, LOW)
    cum_end = cum[:, T - 1 :]
    cm_end = cm[:, T - 1 :]
    sc_own[0:8] = jnp.broadcast_to(cum_end + cm_end, (8, 128))
    sc_own[8:16] = jnp.broadcast_to(cum_end, (8, 128))
    cm_t = jnp.transpose(cm)
    key_scale = jnp.exp(g - cm_end)

    pl.semaphore_wait(barrier, len(greet))
    halo_copy = remote(
        conv_hbm.at[pl.ds(T - 16, 16)], halo, (halo_sem.at[0], halo_sem.at[1]), after
    )
    halo_copy.start()
    sc_copy = remote(sc_own, sc_other, (sc_sem.at[0], sc_sem.at[1]), other)
    sc_copy.start()

    loads[1].wait()
    loads[2].wait()
    loads[3].wait()
    rows = 64

    def widen(i, _):
        r = pl.multiple_of(i * rows, rows)
        xpad[pl.ds(r + 8, rows), :] = conv_v[pl.ds(r, rows), :].astype(F32)
        return 0

    lax.fori_loop(0, T // rows, widen, 0)

    def conv(i, _):
        r = pl.multiple_of(i * rows, rows)
        ext = xpad[pl.ds(r, rows + 8), :]
        pre = cb[0:1, :] + cw[0:1, :] * ext[5 : 5 + rows]
        for j in range(1, 4):
            pre = pre + cw[j : j + 1, :] * ext[5 + j : 5 + j + rows]
        act[pl.ds(r, rows), :] = (pre / (1.0 + jnp.exp(-pre))).astype(BF16)
        return 0

    lax.fori_loop(1, T // rows, conv, 0)
    halo_copy.wait()
    edge = halo[...].astype(F32)[8:16]
    xpad[0:8, :] = jnp.where(me > 0, edge, 0.0)
    conv(0, 0)

    sc_copy.wait()
    is_first = core == 0
    own_m, own_d = sc_own[0:8], sc_own[8:16]
    oth_m, oth_d = sc_other[0:8], sc_other[8:16]
    m0 = jnp.where(is_first, own_m, oth_m)
    d0 = jnp.where(is_first, own_d, oth_d)
    m1 = jnp.where(is_first, oth_m, own_m)
    d1 = jnp.where(is_first, oth_d, own_d)
    chip_m, chip_d = join((m0, d0), (m1, d1))
    mine = jnp.concatenate([chip_m, chip_d], axis=0)
    sc_chip[z] = mine
    scz = []
    for k in range(1, nz):
        copy = remote(sc_chip.at[z], sc_chip.at[z], (scz_sem.at[0, k], scz_sem.at[1, k]), z_peer(k))
        copy.start()
        scz.append(copy)

    loads[4].wait()
    loads[5].wait()

    def project(h):
        col = pl.multiple_of(h * DK, DK)
        a = act[:, pl.ds(col, DK)]
        q[h] = dot(a, qk[0, h]).astype(BF16)
        kt[h] = (
            lax.dot_general(qk[1, h], a, (((0,), (1,)), ((), ())), preferred_element_type=F32)
            * (1.0 / 16.0)
        ).astype(BF16)

    def block_state(h, scale):
        col = pl.multiple_of(h * DV, DV)
        scaled = (kt[h].astype(F32) * scale).astype(BF16)
        return dot(scaled, val[:, pl.ds(col, DV)])

    scale_own = jnp.where(is_first, key_scale[0:1], key_scale[1:2])
    scale_oth = jnp.where(is_first, key_scale[1:2], key_scale[0:1])
    project(1 - core)
    st_send[...] = block_state(1 - core, scale_oth).astype(BF16)
    st_copy = remote(st_send, st_recv, (st_sem.at[0], st_sem.at[1]), other)
    st_copy.start()
    project(core)
    state[...] = block_state(core, scale_own)

    for copy in scz:
        copy.wait()
    row_m, row_d = jnp.full((8, 128), LOW, F32), jnp.zeros((8, 128), F32)
    pre_m, pre_d = [], []
    for k in range(nz):
        pre_m.append(row_m)
        pre_d.append(row_d)
        row_m, row_d = join((row_m, row_d), (sc_chip[k, 0:8], sc_chip[k, 8:16]))
    sc_row[x] = jnp.concatenate([row_m, row_d], axis=0)
    scx = []
    for k in range(1, nx):
        copy = remote(sc_row.at[x], sc_row.at[x], (scx_sem.at[0, k], scx_sem.at[1, k]), x_peer(k))
        copy.start()
        scx.append(copy)

    def head_of(tile):
        return jnp.where(is_first, tile[0:1, 0:1], tile[1:2, 0:1])

    st_copy.wait()
    own_factor = jnp.where(is_first, jnp.exp(m0 + d1 - chip_m), jnp.exp(m1 - chip_m))
    oth_factor = jnp.where(is_first, jnp.exp(m1 - chip_m), jnp.exp(m0 + d1 - chip_m))
    own_factor, oth_factor = head_of(own_factor), head_of(oth_factor)

    def pack(i, _):
        r = pl.multiple_of(i * slice_rows, slice_rows)
        mixed = (
            state[pl.ds(r, slice_rows), :] * own_factor
            + st_recv[pl.ds(r, slice_rows), :].astype(F32) * oth_factor
        )
        t_send[i] = mixed.astype(BF16)
        return 0

    lax.fori_loop(0, nz, pack, 0)
    tz = []
    for k in range(1, nz):
        to = lax.rem(z + k, nz)
        copy = remote(t_send.at[to], t_in.at[z], (tz_sem.at[0, k], tz_sem.at[1, k]), z_peer(k))
        copy.start()
        tz.append(copy)
    t_in[z] = t_send[z]

    def inner(h):
        for part in range(2):
            lo, hi = part * HALF, (part + 1) * HALF
            scores = dot(q[h, lo:hi, :], kt[h, :, 0:hi])
            row = lax.broadcasted_iota(jnp.int32, (HALF, hi), 0) + lo
            col = lax.broadcasted_iota(jnp.int32, (HALF, hi), 1)
            gap = jnp.where(row >= col, g[h : h + 1, 0:hi] - cm_t[lo:hi, h : h + 1], LOW)
            weights = (scores * jnp.exp(gap)).astype(BF16)
            local[h, lo:hi, :] = dot(weights, val[0:hi, h * DV : (h + 1) * DV])

    inner(0)
    inner(1)

    for copy in scx:
        copy.wait()
    for copy in tz:
        copy.wait()
    run = jnp.zeros((slice_rows, DV), F32)
    before_chip = []
    for k in range(nz):
        before_chip.append(run)
        nm, nd = (row_m, row_d) if k == nz - 1 else (pre_m[k + 1], pre_d[k + 1])
        keep = head_of(jnp.exp(pre_m[k] + sc_chip[k, 8:16] - nm))
        add = head_of(jnp.exp(sc_chip[k, 0:8] - nm))
        run = run * keep + t_in[k].astype(F32) * add
        if k < nz - 1:
            c_send[k + 1] = run
    r_send[...] = run.astype(BF16)
    rx = []
    for k in range(1, nx):
        copy = remote(r_send, r_in.at[x], (rx_sem.at[0, k], rx_sem.at[1, k]), x_peer(k))
        copy.start()
        rx.append(copy)
    r_in[x] = r_send[...]
    x_m, x_d = jnp.full((8, 128), LOW, F32), jnp.zeros((8, 128), F32)
    x_keep, x_add = [], []
    for k in range(nx):
        late = (
            jnp.where(k < x, sc_row[k, 0:8], LOW),
            jnp.where(k < x, sc_row[k, 8:16], 0.0),
        )
        nm, nd = join((x_m, x_d), late)
        x_keep.append(head_of(jnp.exp(x_m + late[1] - nm)))
        x_add.append(head_of(jnp.where(k < x, jnp.exp(late[0] - nm), 0.0)))
        x_m, x_d = nm, nd
    for copy in rx:
        copy.wait()
    total = jnp.zeros((slice_rows, DV), F32)
    for k in range(nx):
        total = total * x_keep[k] + r_in[k].astype(F32) * x_add[k]

    chip_carry_m = jnp.full((8, 128), LOW, F32)
    cz = []
    for k in range(nz):
        ahead = x_m + pre_d[k]
        cm_k = jnp.maximum(ahead, pre_m[k])
        chip_carry_m = jnp.where(z == k, cm_k, chip_carry_m)
        carried = total * head_of(jnp.exp(ahead - cm_k))
        if k > 0:
            carried = carried + c_send[k] * head_of(jnp.exp(pre_m[k] - cm_k))
        t_send[k] = carried.astype(BF16)
    for k in range(1, nz):
        to = lax.rem(z + k, nz)
        copy = remote(t_send.at[to], c_in.at[z], (cz_sem.at[0, k], cz_sem.at[1, k]), z_peer(k))
        copy.start()
        cz.append(copy)
    c_in[z] = t_send[z]

    second_m = jnp.maximum(chip_carry_m + d0, m0)
    from_chip = jnp.exp(chip_carry_m + d0 - second_m)
    from_first = jnp.exp(m0 - second_m)
    carry_m = jnp.where(is_first, chip_carry_m, second_m)
    own_a = head_of(jnp.where(is_first, 1.0, from_chip))
    own_b = head_of(jnp.where(is_first, 0.0, from_first))
    oth_a = head_of(jnp.where(is_first, from_chip, 1.0))
    oth_b = head_of(jnp.where(is_first, from_first, 0.0))
    for copy in cz:
        copy.wait()

    def spread(i, _):
        r = pl.multiple_of(i * slice_rows, slice_rows)
        piece = c_in[i].astype(F32)
        first = jnp.where(
            is_first, state[pl.ds(r, slice_rows), :], st_recv[pl.ds(r, slice_rows), :].astype(F32)
        )
        p_send[pl.ds(r, slice_rows), :] = (piece * oth_a + first * oth_b).astype(BF16)
        carry[core, pl.ds(r, slice_rows), :] = (piece * own_a + first * own_b).astype(BF16)
        return 0

    lax.fori_loop(0, nz, spread, 0)
    p_copy = remote(p_send, carry.at[core], (p_sem.at[0], p_sem.at[1]), other)
    p_copy.start()
    loads[6].wait()
    loads[7].wait()
    p_copy.wait()

    def norm(part):
        lo, hi = part * HALF, (part + 1) * HALF
        for h in range(2):
            gap = carry_m[h : h + 1, 0:1] - cm_t[lo:hi, h : h + 1]
            top = jnp.maximum(gap, 0.0)
            total = local[h, lo:hi, :] * jnp.exp(-top) + jnp.exp(gap - top) * dot(
                q[h, lo:hi, :], carry[h]
            )
            scale = lax.rsqrt(jnp.mean(total * total, axis=1, keepdims=True) + 1e-6)
            normed[lo:hi, h * DV : (h + 1) * DV] = (
                total * scale * gain[0:1, h * DV : (h + 1) * DV]
            ).astype(BF16)

    def product(part, k, piece):
        col = pl.multiple_of(y_peer(k) * COLS + piece * PIECE, PIECE)
        return dot(normed[part * HALF : (part + 1) * HALF, :], w[:, pl.ds(col, PIECE)])

    far = (NY - 1, 1)

    def two_copy(side, p):
        return remote(two_s.at[side, p], two_r.at[side, p],
                      (two_sem.at[0, side, p], two_sem.at[1, side, p]), me, y_peer(far[side]))

    def dir_copy(side, p):
        return remote(dir_s.at[side, p], dir_r.at[side, p],
                      (dir_sem.at[0, side, p], dir_sem.at[1, side, p]), me, y_peer(far[side]))

    def rel_copy(side, p):
        return remote(rel_s.at[side, p], rel_r.at[side, p],
                      (rel_sem.at[0, side, p], rel_sem.at[1, side, p]), me, y_peer(far[side]))

    def each(fn):
        def step(p, _):
            fn(p)
            return 0

        lax.fori_loop(0, PIECES, step, 0)

    for side in range(2):
        norm(side)

        def two(p, side=side):
            two_s[side, p] = product(side, 2, p).astype(BF16)
            two_copy(side, p).start()

        each(two)
    for side in range(2):

        def direct(p, side=side):
            dir_s[side, p] = product(1 - side, far[side], p).astype(BF16)
            dir_copy(side, p).start()

        each(direct)
    for side in range(2):

        def relay(p, side=side):
            mine = product(side, far[side], p)
            two_copy(side, p).wait_recv()
            rel_s[side, p] = (mine + two_r[side, p].astype(F32)).astype(BF16)
            rel_copy(side, p).start()

        each(relay)
    for side in range(2):

        def keep(p, side=side):
            acc[side, p] = product(side, 0, p)

        each(keep)
    for side in range(2):

        def add(p, side=side):
            dir_copy(1 - side, p).wait_recv()
            acc[side, p] = acc[side, p] + dir_r[1 - side, p].astype(F32)

        each(add)

    def finish(p):
        for side in range(2):
            rel_copy(side, p).wait_recv()
            col = pl.multiple_of(p * PIECE, PIECE)
            out_v[side * HALF : (side + 1) * HALF, pl.ds(col, PIECE)] = (
                acc[side, p] + rel_r[side, p].astype(F32)
            ).astype(BF16)

    each(finish)
    out_copy = pltpu.make_async_copy(out_v, out_hbm, out_sem)
    out_copy.start()

    def drain(p):
        for side in range(2):
            two_copy(side, p).wait_send()
            dir_copy(side, p).wait_send()
            rel_copy(side, p).wait_send()

    each(drain)
    out_copy.wait()


def solution(mesh):
    n_ctx = mesh.shape["ctx"]
    nx, nz = {64: (4, 8), 8: (2, 2), 16: (2, 4)}[n_ctx]
    slice_rows = DK // nz

    def body(conv_in, conv_weight, conv_bias, qk_weight, value_in, gate_pre, norm_gain, out_weight):
        dma = pltpu.SemaphoreType.DMA
        vmem = pltpu.VMEM
        return pl.pallas_call(
            functools.partial(body_kernel, nx, nz),
            out_shape=jax.ShapeDtypeStruct((T, COLS), BF16),
            in_specs=[pl.BlockSpec(memory_space=pl.ANY)] * 8,
            out_specs=pl.BlockSpec(memory_space=pl.ANY),
            scratch_shapes=[
                vmem((T, 2 * DK), BF16),
                vmem((4, 2 * DK), F32),
                vmem((1, 2 * DK), F32),
                vmem((2, 2, DK, DK), BF16),
                vmem((T, 2 * DV), BF16),
                vmem((2, 2, T), F32),
                vmem((1, 2 * DV), F32),
                vmem((2 * DV, DM), BF16),
                vmem((T + 8, 2 * DK), F32),
                vmem((16, 2 * DK), BF16),
                vmem((T, 2 * DK), BF16),
                vmem((2, T, DK), BF16),
                vmem((2, DK, T), BF16),
                vmem((DK, DV), F32),
                vmem((2, T, DV), F32),
                vmem((16, 128), F32),
                vmem((16, 128), F32),
                vmem((nz, 16, 128), F32),
                vmem((nx, 16, 128), F32),
                vmem((DK, DV), BF16),
                vmem((DK, DV), BF16),
                vmem((nz, slice_rows, DV), BF16),
                vmem((nz, slice_rows, DV), BF16),
                vmem((slice_rows, DV), BF16),
                vmem((nx, slice_rows, DV), BF16),
                vmem((nz, slice_rows, DV), F32),
                vmem((nz, slice_rows, DV), BF16),
                vmem((DK, DV), BF16),
                vmem((2, DK, DV), BF16),
                vmem((T, 2 * DV), BF16),
                vmem((2, PIECES, HALF, PIECE), F32),
            ]
            + [vmem((2, PIECES, HALF, PIECE), BF16)] * 6
            + [
                vmem((T, COLS), BF16),
                dma((8,)),
                dma((2,)),
                dma((2,)),
                dma((2, nz)),
                dma((2, nx)),
                dma((2,)),
                dma((2, nz)),
                dma((2, nx)),
                dma((2, nz)),
                dma((2,)),
                dma((2, 2, PIECES)),
                dma((2, 2, PIECES)),
                dma((2, 2, PIECES)),
                dma,
            ],
            compiler_params=pltpu.CompilerParams(
                collective_id=0, has_side_effects=True, vmem_limit_bytes=56 * 1024 * 1024
            ),
        )(
            conv_in, conv_weight, conv_bias.reshape(1, -1), qk_weight, value_in, gate_pre,
            norm_gain.reshape(1, -1), out_weight,
        )

    return jax.shard_map(
        body,
        mesh=mesh,
        in_specs=(
            P("ctx", "head"),
            P(None, "head"),
            P("head"),
            P(None, "head", None, None),
            P("ctx", "head"),
            P(None, "head", "ctx"),
            P("head"),
            P("head", None),
        ),
        out_specs=P("ctx", "head"),
        check_vma=False,
    )
```

time: 443 us -> 84.4 us (0.19)
  waiting for transfers between devices: 221 us -> 0 us
  blocking collectives: 167 us -> 0 us
  Pallas kernels: 0 us -> 82 us
  matrix products: 20.7 us -> 0 us
  between operations: 14.3 us -> 0.01 us
  other arithmetic: 7.42 us -> 0 us
  starting transfers between devices: 4.97 us -> 0 us
    reduce_scatter x1 -> x0, waiting for transfers between devices: 155 us -> none  [body(): lax.psum_scatter(partial_value.astype(jnp.bfloat16), 'head', scatter_dime...]
    unnamed x1 -> x0, blocking collectives: 127 us -> none
    pallas_call x0 -> x1, Pallas kernels: none -> 82 us  [body(): pl.pallas_call(functools.partial(body_kernel, nx, nz), out_shape=jax.Shap...]
    all_gather x1 -> x0, waiting for transfers between devices: 66.6 us -> none  [prefix(): gathered = jax.tree.map(lambda a: lax.all_gather(a, axis), part)]
    all_gather x1 -> x0, blocking collectives: 39.6 us -> none  [prefix(): gathered = jax.tree.map(lambda a: lax.all_gather(a, axis), part)]
    dot_general x7 -> x0, matrix products: 20.7 us -> none  [the longest x1 9.48 us: body(): jnp.dot(normed, out_weight, preferred_element_type=jnp.float32)]
    ppermute x1 -> x0, starting transfers between devices: 4.92 us -> none  [from_behind(): return lax.ppermute(block, axis, route)]
  transfers between devices with their start and end apart: 3 -> 0, of which waited for: 2 -> 0; matrix products, arithmetic and copies ran while one was open for 3% -> 0% of each run, Pallas kernels for 0% -> 0%
where the time goes in v1:
time: 84.4 us; the launch traced here: 84.3 us
  Pallas kernels  82 us (97%)
  local copies, waits for them, and re-layouts  2.26 us (3%)
    pallas_call x1, Pallas kernels, body(): pl.pallas_call(functools.partial(body_kernel, nx, nz), out_shape=jax.Shap...  82 us
    unnamed x1, local copies, waits for them, and re-layouts  2.26 us

profile of v1, /device:TPU:1, one launch (start us, length us, event | category | flops | bytes accessed | tf_op | source)
XLA Modules:
  0.0 84.3 jit_solution(4550769340909039348)
XLA Ops:
  0.0 82.0 %shard_map.82 = bf16[512,1024]{1,0:T(8,128)(2,1)} custom-call(bf16[512,512]{1,0:T(8,128)(2,1)} %conv_hbm.1, f32[4,512]{1,0:T(4,128)} %cw_hbm.1, f32[1,512]{1,0:T(1,128)} %bitcast.3, bf16[2,2,256,256]{3,2,1,0:T(8,128)(2,1)} %qk_hbm.1, bf16[512,1024]{1,0:T(8,128)(2,1)} %val_hbm.1, f32[2,2,512]{2,1,0:T(2,128)} %gate_hbm.1, f32[1,1024]{1,0:T(1,128)} %bitcast.2, ...), custom_call_target="tpu_custom_call" | custom-call | tf_op jit(solution)/shard_map/pallas_call | solution.py:436
  82.0 2.3 %copy.10 = bf16[512,1024]{1,0:T(8,128)(2,1)} copy(bf16[512,1024]{1,0:T(8,128)(2,1)} %shard_map.82) | data formatting | bytes 2097152

commit v2 on v1

v2 whole, which is shorter than its diff:
```python
import jax
import jax.numpy as jnp
from jax import lax
from jax.experimental import pallas as pl
from jax.experimental.pallas import tpu as pltpu
from jax.sharding import PartitionSpec as P

MESH = pl.DeviceIdType.MESH
F32 = jnp.float32
BF16 = jnp.bfloat16
LOW = -1e30

T = 512
HALF = 256
DK = 256
DV = 512
DM = 4096
FAR_FIRST = (4, 3, 5, 2, 6, 1, 7)
NX, NZ, NY = 4, 8, 4
COLS = DM // NY
ROWS = 64
PIECES = T // ROWS
LATE = 128
AHEAD = 2
LAG = 2


def dot(a, b):
    return jnp.dot(a, b, preferred_element_type=F32)


def scan_lanes(v, combine, fill):
    lane = lax.broadcasted_iota(jnp.int32, v.shape, 1)
    shift = 1
    while shift < v.shape[1]:
        moved = pltpu.roll(v, shift, 1)
        v = combine(v, jnp.where(lane >= shift, moved, fill))
        shift *= 2
    return v


def join(early, late):
    return jnp.maximum(early[0] + late[1], late[0]), early[1] + late[1]


def body_kernel(
    conv_hbm, cw_hbm, cb_hbm, qk_hbm, val_hbm, gate_hbm, gain_hbm, w_hbm,
    out_hbm,
    conv_v, cw, cb, qk, val, gate, gain, w, xpad, halo, act, q, kt, state, state_oth, local,
    sc_own, sc_other, sc_chip, sc_row, st_send, st_recv, t_send, t_in, r_send, r_in,
    c_send, c_factor, c_in, p_send, carry, cm_col, normed, normed_in, acc, part_s, part_r, w_far, out_v,
    ld_sem, halo_sem, sc_sem, scz_sem, scx_sem, st_sem, tz_sem, rx_sem, cz_sem, p_sem,
    wy_sem, wx_sem, wh_sem, wc_sem, ag_sem, rs_sem, out_sem,
):
    nx, nz = NX, NZ
    n_ctx = nx * nz * 2
    slice_rows = DK // nz
    me = lax.axis_index("ctx")
    y = lax.axis_index("head")
    core = lax.rem(me, 2)
    chip = lax.div(me, 2)
    z = lax.rem(chip, nz)
    x = lax.div(chip, nz)
    other = me + 1 - 2 * core

    def z_peer(k):
        return (x * nz + lax.rem(z + k, nz)) * 2 + core

    def x_peer(k):
        return (lax.rem(x + k, nx) * nz + z) * 2 + core

    pair = y + 1 - 2 * lax.rem(y, 2)
    mate = NY - 1 - y

    def remote(src, dst, sems, to, at_y=None):
        return pltpu.make_async_remote_copy(
            src_ref=src, dst_ref=dst, send_sem=sems[0], recv_sem=sems[1],
            device_id=(to, y if at_y is None else at_y), device_id_type=MESH,
        )

    loads = [
        pltpu.make_async_copy(src, dst, ld_sem.at[i])
        for i, (src, dst) in enumerate(
            [(gate_hbm, gate), (conv_hbm, conv_v), (cw_hbm, cw), (cb_hbm, cb),
             (qk_hbm, qk), (val_hbm, val), (gain_hbm, gain),
             (w_hbm.at[:, pl.ds(pl.multiple_of(mate * COLS, COLS), COLS)], w.at[0]),
             (w_hbm.at[:, pl.ds(pl.multiple_of(y * COLS, COLS), COLS)], w.at[1])]
        )
    ]
    for load in loads:
        load.start()

    barrier = pltpu.get_barrier_semaphore()
    after = lax.rem(me + 1, n_ctx)
    before = lax.rem(me + n_ctx - 1, n_ctx)
    greet = [(after, y), (before, y), (other, y)]
    greet += [(z_peer(k), y) for k in range(1, nz)]
    greet += [(x_peer(k), y) for k in range(1, nx)]
    greet += [(me, pair), (me, mate)]
    for to in greet:
        pl.semaphore_signal(barrier, inc=1, device_id=to, device_id_type=MESH)

    loads[0].wait()
    pad = jnp.zeros((6, T), F32)
    in_gate = jnp.concatenate([gate[0], pad], axis=0)
    forget = jnp.concatenate([gate[1], pad], axis=0)
    log_forget = jnp.minimum(forget, 0.0) - jnp.log1p(jnp.exp(-jnp.abs(forget)))
    cum = scan_lanes(log_forget, jnp.add, 0.0)
    g = in_gate - cum
    cm = scan_lanes(g, jnp.maximum, LOW)
    cum_end = cum[:, T - 1 :]
    cm_end = cm[:, T - 1 :]
    sc_own[0:8] = jnp.broadcast_to(cum_end + cm_end, (8, 128))
    sc_own[8:16] = jnp.broadcast_to(cum_end, (8, 128))
    cm_t = jnp.transpose(cm)
    cm_col[:, 0:8] = cm_t
    key_scale = jnp.exp(g - cm_end)

    pl.semaphore_wait(barrier, len(greet))
    halo_copy = remote(
        conv_hbm.at[pl.ds(T - 16, 16)], halo, (halo_sem.at[0], halo_sem.at[1]), after
    )
    halo_copy.start()
    sc_copy = remote(sc_own, sc_other, (sc_sem.at[0], sc_sem.at[1]), other)
    sc_copy.start()

    w_rows = 2 * DV // (2 * nx)

    def w_piece(j, at_x, lo=0, count=w_rows):
        row = pl.multiple_of((lax.rem(at_x + nx, nx) * 2 + core) * w_rows + lo, 16)
        return w_far.at[j, pl.ds(row, count), :]

    def wy_copy(j):
        column = pl.multiple_of((NY - 1 - pair if j == 0 else pair) * COLS, COLS)
        row = pl.multiple_of((x * 2 + core) * w_rows, w_rows)
        return remote(w_hbm.at[pl.ds(row, w_rows), pl.ds(column, COLS)], w_piece(j, x),
                      (wy_sem.at[0, j], wy_sem.at[1, j]), me, pair)

    def wx_copy(j, side):
        piece = w_piece(j, x)
        return remote(piece, piece, (wx_sem.at[0, j, side], wx_sem.at[1, j, side]), x_peer((1, nx - 1)[side]))

    def wh_copy(j, side):
        piece = w_piece(j, x + (-1, 1)[side], side * (w_rows // 2), w_rows // 2)
        return remote(piece, piece, (wh_sem.at[0, j, side], wh_sem.at[1, j, side]), x_peer((1, nx - 1)[side]))

    def wc_copy(j, k):
        piece = w_piece(j, x + k)
        return remote(piece, piece, (wc_sem.at[0, j, k], wc_sem.at[1, j, k]), other)

    def w_first(j):
        wy_copy(j).wait_recv()
        wx_copy(j, 0).start()
        wx_copy(j, 1).start()
        wc_copy(j, 0).start()
        if j == 0:
            wy_copy(1).start()

    def w_second(j):
        for side in range(2):
            wx_copy(j, side).wait_recv()
            wh_copy(j, side).start()
            wc_copy(j, (nx - 1, 1)[side]).start()

    def w_third(j):
        for side in range(2):
            wh_copy(j, side).wait_recv()
        wc_copy(j, 2).start()

    def w_wait(j):
        for k in range(nx):
            wc_copy(j, k).wait()

    def w_drain(j):
        wy_copy(j).wait_send()
        for side in range(2):
            wx_copy(j, side).wait_send()
            wh_copy(j, side).wait_send()

    wy_copy(0).start()

    loads[1].wait()
    loads[2].wait()
    loads[3].wait()
    rows = 64

    def widen(i, _):
        r = pl.multiple_of(i * rows, rows)
        xpad[pl.ds(r + 8, rows), :] = conv_v[pl.ds(r, rows), :].astype(F32)
        return 0

    lax.fori_loop(0, T // rows, widen, 0)

    def conv(i, _):
        r = pl.multiple_of(i * rows, rows)
        ext = xpad[pl.ds(r, rows + 8), :]
        pre = cb[0:1, :] + cw[0:1, :] * ext[5 : 5 + rows]
        for j in range(1, 4):
            pre = pre + cw[j : j + 1, :] * ext[5 + j : 5 + j + rows]
        act[pl.ds(r, rows), :] = (pre / (1.0 + jnp.exp(-pre))).astype(BF16)
        return 0

    lax.fori_loop(LATE // rows, T // rows, conv, 0)

    loads[4].wait()
    loads[5].wait()

    def project(h, lo, hi):
        col = pl.multiple_of(h * DK, DK)
        a = act[lo:hi, pl.ds(col, DK)]
        q[h, lo:hi, :] = dot(a, qk[0, h]).astype(BF16)
        kt[h, :, lo:hi] = (
            lax.dot_general(qk[1, h], a, (((0,), (1,)), ((), ())), preferred_element_type=F32)
            * (1.0 / 16.0)
        ).astype(BF16)

    def block_state(h, scale, lo, hi):
        col = pl.multiple_of(h * DV, DV)
        scaled = (kt[h, :, lo:hi].astype(F32) * scale[:, lo:hi]).astype(BF16)
        return dot(scaled, val[lo:hi, pl.ds(col, DV)])

    is_first = core == 0
    scale_own = jnp.where(is_first, key_scale[0:1], key_scale[1:2])
    scale_oth = jnp.where(is_first, key_scale[1:2], key_scale[0:1])
    project(1 - core, LATE, T)
    state_oth[...] = block_state(1 - core, scale_oth, LATE, T)
    project(core, LATE, T)
    state[...] = block_state(core, scale_own, LATE, T)

    halo_copy.wait()
    edge = halo[...].astype(F32)[8:16]
    xpad[0:8, :] = jnp.where(me > 0, edge, 0.0)
    lax.fori_loop(0, LATE // rows, conv, 0)
    project(1 - core, 0, LATE)
    st_send[...] = (state_oth[...] + block_state(1 - core, scale_oth, 0, LATE)).astype(BF16)
    st_copy = remote(st_send, st_recv, (st_sem.at[0], st_sem.at[1]), other)
    st_copy.start()
    project(core, 0, LATE)
    state[...] = state[...] + block_state(core, scale_own, 0, LATE)

    sc_copy.wait()
    own_m, own_d = sc_own[0:8], sc_own[8:16]
    oth_m, oth_d = sc_other[0:8], sc_other[8:16]
    m0 = jnp.where(is_first, own_m, oth_m)
    d0 = jnp.where(is_first, own_d, oth_d)
    m1 = jnp.where(is_first, oth_m, own_m)
    d1 = jnp.where(is_first, oth_d, own_d)
    chip_m, chip_d = join((m0, d0), (m1, d1))
    mine = jnp.concatenate([chip_m, chip_d], axis=0)
    sc_chip[z] = mine
    scz = []
    for k in range(1, nz):
        copy = remote(sc_chip.at[z], sc_chip.at[z], (scz_sem.at[0, k], scz_sem.at[1, k]), z_peer(k))
        copy.start()
        scz.append(copy)

    def head_of(tile):
        row = jnp.where(is_first, tile[0:1], tile[1:2])
        return jnp.concatenate([row] * (DV // 128), axis=1)

    st_copy.wait()
    own_factor = jnp.where(is_first, jnp.exp(m0 + d1 - chip_m), jnp.exp(m1 - chip_m))
    oth_factor = jnp.where(is_first, jnp.exp(m1 - chip_m), jnp.exp(m0 + d1 - chip_m))
    own_factor, oth_factor = head_of(own_factor), head_of(oth_factor)

    def slice_of(i):
        return pl.ds(pl.multiple_of(i * slice_rows, slice_rows), slice_rows)

    def pack(i):
        mixed = state[slice_of(i), :] * own_factor + st_recv[slice_of(i), :].astype(F32) * oth_factor
        return mixed.astype(BF16)

    tz = []
    for k in FAR_FIRST:
        to = lax.rem(z + k, nz)
        t_send[to] = pack(to)
        copy = remote(t_send.at[to], t_in.at[z], (tz_sem.at[0, k], tz_sem.at[1, k]), z_peer(k))
        copy.start()
        tz.append(copy)
    t_in[z] = pack(z)
    w_first(0)

    for copy in scz:
        copy.wait()
    row_m, row_d = jnp.full((8, 128), LOW, F32), jnp.zeros((8, 128), F32)
    pre_m, pre_d = [], []
    for k in range(nz):
        pre_m.append(row_m)
        pre_d.append(row_d)
        row_m, row_d = join((row_m, row_d), (sc_chip[k, 0:8], sc_chip[k, 8:16]))
    sc_row[x] = jnp.concatenate([row_m, row_d], axis=0)
    scx = []
    for k in range(1, nx):
        copy = remote(sc_row.at[x], sc_row.at[x], (scx_sem.at[0, k], scx_sem.at[1, k]), x_peer(k))
        copy.start()
        scx.append(copy)

    def inner(h):
        for part in range(2):
            lo, hi = part * HALF, (part + 1) * HALF
            scores = dot(q[h, lo:hi, :], kt[h, :, 0:hi])
            row = lax.broadcasted_iota(jnp.int32, (HALF, hi), 0) + lo
            col = lax.broadcasted_iota(jnp.int32, (HALF, hi), 1)
            gap = jnp.where(row >= col, g[h : h + 1, 0:hi] - cm_t[lo:hi, h : h + 1], LOW)
            weights = (scores * jnp.exp(gap)).astype(BF16)
            local[h, lo:hi, :] = dot(weights, val[0:hi, h * DV : (h + 1) * DV])

    inner(0)
    inner(1)

    to_row = []
    m, d = jnp.full((8, 128), LOW, F32), jnp.zeros((8, 128), F32)
    for k in reversed(range(nz)):
        to_row.insert(0, head_of(jnp.exp(sc_chip[k, 0:8] + d - row_m)))
        d = d + sc_chip[k, 8:16]
    keep, add = [], []
    for k in range(nz - 1):
        keep.append(head_of(jnp.exp(pre_m[k] + sc_chip[k, 8:16] - pre_m[k + 1])))
        add.append(head_of(jnp.exp(sc_chip[k, 0:8] - pre_m[k + 1])))
    for copy in tz:
        copy.wait()
    row_sum = t_in[0].astype(F32) * to_row[0]
    for k in range(1, nz):
        row_sum = row_sum + t_in[k].astype(F32) * to_row[k]
    r_send[...] = row_sum.astype(BF16)
    rx = []
    for k in (2, 1, 3):
        copy = remote(r_send, r_in.at[x], (rx_sem.at[0, k], rx_sem.at[1, k]), x_peer(k))
        copy.start()
        rx.append(copy)
    r_in[x] = r_send[...]
    w_first(1)
    run = t_in[0].astype(F32) * add[0]
    c_send[1] = run
    for k in range(1, nz - 1):
        run = run * keep[k] + t_in[k].astype(F32) * add[k]
        c_send[k + 1] = run
    for copy in scx:
        copy.wait()
    x_m, x_d = jnp.full((8, 128), LOW, F32), jnp.zeros((8, 128), F32)
    x_keep, x_add = [], []
    for k in range(nx):
        late = (
            jnp.where(k < x, sc_row[k, 0:8], LOW),
            jnp.where(k < x, sc_row[k, 8:16], 0.0),
        )
        nm, nd = join((x_m, x_d), late)
        x_keep.append(head_of(jnp.exp(x_m + late[1] - nm)))
        x_add.append(head_of(jnp.where(k < x, jnp.exp(late[0] - nm), 0.0)))
        x_m, x_d = nm, nd
    chip_carry_m = jnp.full((8, 128), LOW, F32)
    for k in range(nz):
        ahead = x_m + pre_d[k]
        cm_k = jnp.maximum(ahead, pre_m[k])
        chip_carry_m = jnp.where(z == k, cm_k, chip_carry_m)
        c_factor[0, k] = jnp.broadcast_to(head_of(jnp.exp(ahead - cm_k)), (8, DV))
        c_factor[1, k] = jnp.broadcast_to(head_of(jnp.exp(pre_m[k] - cm_k)), (8, DV))
    c_send[0] = jnp.zeros((slice_rows, DV), F32)

    second_m = jnp.maximum(chip_carry_m + d0, m0)
    from_chip = jnp.exp(chip_carry_m + d0 - second_m)
    from_first = jnp.exp(m0 - second_m)
    carry_m = jnp.where(is_first, chip_carry_m, second_m)
    own_a = head_of(jnp.where(is_first, 1.0, from_chip))
    own_b = head_of(jnp.where(is_first, 0.0, from_first))
    oth_a = head_of(jnp.where(is_first, from_chip, 1.0))
    oth_b = head_of(jnp.where(is_first, from_first, 0.0))

    for copy in rx:
        copy.wait()
    total = r_in[0].astype(F32) * x_add[0]
    for k in range(1, nx):
        total = total * x_keep[k] + r_in[k].astype(F32) * x_add[k]

    def carried(i):
        return (total * c_factor[0, i, 0:1] + c_send[i] * c_factor[1, i, 0:1]).astype(BF16)

    cz = {}
    for k in FAR_FIRST:
        to = lax.rem(z + k, nz)
        t_send[to] = carried(to)
        copy = remote(t_send.at[to], c_in.at[z], (cz_sem.at[0, k], cz_sem.at[1, k]), z_peer(k))
        copy.start()
        cz[k] = copy
    c_in[z] = carried(z)
    w_second(0)

    def p_copy(k):
        at = slice_of(lax.rem(z + nz - k, nz))
        return remote(p_send.at[at], carry.at[core, at], (p_sem.at[0, k], p_sem.at[1, k]), other)

    def p_arrival(k):
        at = slice_of(lax.rem(z + nz - k, nz))
        return remote(p_send.at[at], carry.at[1 - core, at], (p_sem.at[0, k], p_sem.at[1, k]), other)

    def spread(k):
        i = lax.rem(z + nz - k, nz)
        piece = c_in[i].astype(F32)
        first = jnp.where(is_first, state[slice_of(i), :], st_recv[slice_of(i), :].astype(F32))
        p_send[slice_of(i), :] = (piece * oth_a + first * oth_b).astype(BF16)
        carry[core, slice_of(i), :] = (piece * own_a + first * own_b).astype(BF16)
        p_copy(k).start()

    spread(0)
    for k in reversed(FAR_FIRST):
        cz[k].wait_recv()
        spread(k)
    for k in FAR_FIRST:
        cz[k].wait_send()
    loads[6].wait()
    loads[7].wait()
    loads[8].wait()
    w_third(0)
    for k in range(nz):
        p_copy(k).wait_send()
        p_arrival(k).wait_recv()

    def token(i):
        return pl.ds(pl.multiple_of(i * ROWS, ROWS), ROWS)

    def norm(i):
        at = token(i)
        column = cm_col[at, :]
        for h in range(2):
            gap = carry_m[h : h + 1, 0:1] - column[:, h : h + 1]
            top = jnp.maximum(gap, 0.0)
            total = local[h, at, :] * jnp.exp(-top) + jnp.exp(gap - top) * dot(q[h, at, :], carry[h])
            scale = lax.rsqrt(jnp.mean(total * total, axis=1, keepdims=True) + 1e-6)
            normed[at, h * DV : (h + 1) * DV] = (
                total * scale * gain[0:1, h * DV : (h + 1) * DV]
            ).astype(BF16)

    def ag_copy(i):
        return remote(normed.at[token(i)], normed_in.at[token(i)], (ag_sem.at[0, i], ag_sem.at[1, i]), me, pair)

    def rs_copy(i):
        return remote(part_s.at[i], part_r.at[i], (rs_sem.at[0, i], rs_sem.at[1, i]), me, mate)

    def out_copy(i):
        return pltpu.make_async_copy(out_v.at[token(i)], out_hbm.at[token(i)], out_sem.at[i])

    def each(lo, hi, fn):
        def step(i, _):
            fn(i)
            return 0

        lax.fori_loop(lo, hi, step, 0)

    def norm_and_send(i):
        norm(i)
        ag_copy(i).start()

    each(0, AHEAD, norm_and_send)
    each(AHEAD, PIECES, norm)

    def own(i):
        at = pl.ds(pl.multiple_of(lax.rem(i, 4) * 256, 256), 256)
        acc[lax.div(i, 4), :, at] = dot(normed[...], w[lax.div(i, 4), :, at])

    each(0, 8, own)
    w_second(1)
    w_wait(0)

    def finish(i):
        rs_copy(i).wait_recv()
        total = acc[1, token(i), :] + part_r[i].astype(F32)
        out_v[token(i), :] = total.astype(BF16)
        out_copy(i).start()

    def work(i):
        ag_copy(i).wait_recv()

        @pl.when(i + AHEAD < PIECES)
        def _():
            ag_copy(i).wait_send()
            ag_copy(i + AHEAD).start()

        far = normed_in[token(i), :]
        part_s[i] = (acc[0, token(i), :] + dot(far, w_far[0])).astype(BF16)
        rs_copy(i).start()

    each(0, LAG, work)

    def here(i):
        acc[1, token(i), :] = acc[1, token(i), :] + dot(normed_in[token(i), :], w_far[1])

    def both(i):
        work(i)
        here(i - LAG)
        finish(i - LAG)

    w_third(1)
    w_wait(1)
    each(LAG, PIECES, both)
    each(PIECES - LAG, PIECES, here)
    each(PIECES - LAG, PIECES, finish)

    def drain(i):
        rs_copy(i).wait_send()
        out_copy(i).wait()

    each(0, PIECES, drain)
    each(PIECES - AHEAD, PIECES, lambda i: ag_copy(i).wait_send())
    w_drain(0)
    w_drain(1)


def solution(mesh):
    nx, nz = NX, NZ
    slice_rows = DK // nz

    def body(conv_in, conv_weight, conv_bias, qk_weight, value_in, gate_pre, norm_gain, out_weight):
        dma = pltpu.SemaphoreType.DMA
        vmem = pltpu.VMEM
        return pl.pallas_call(
            body_kernel,
            out_shape=jax.ShapeDtypeStruct((T, COLS), BF16),
            in_specs=[pl.BlockSpec(memory_space=pl.ANY)] * 8,
            out_specs=pl.BlockSpec(memory_space=pl.ANY),
            scratch_shapes=[
                vmem((T, 2 * DK), BF16),
                vmem((4, 2 * DK), F32),
                vmem((1, 2 * DK), F32),
                vmem((2, 2, DK, DK), BF16),
                vmem((T, 2 * DV), BF16),
                vmem((2, 2, T), F32),
                vmem((1, 2 * DV), F32),
                vmem((2, 2 * DV, COLS), BF16),
                vmem((T + 8, 2 * DK), F32),
                vmem((16, 2 * DK), BF16),
                vmem((T, 2 * DK), BF16),
                vmem((2, T, DK), BF16),
                vmem((2, DK, T), BF16),
                vmem((DK, DV), F32),
                vmem((DK, DV), F32),
                vmem((2, T, DV), F32),
                vmem((16, 128), F32),
                vmem((16, 128), F32),
                vmem((nz, 16, 128), F32),
                vmem((nx, 16, 128), F32),
                vmem((DK, DV), BF16),
                vmem((DK, DV), BF16),
                vmem((nz, slice_rows, DV), BF16),
                vmem((nz, slice_rows, DV), BF16),
                vmem((slice_rows, DV), BF16),
                vmem((nx, slice_rows, DV), BF16),
                vmem((nz, slice_rows, DV), F32),
                vmem((2, nz, 8, DV), F32),
                vmem((nz, slice_rows, DV), BF16),
                vmem((DK, DV), BF16),
                vmem((2, DK, DV), BF16),
                vmem((T, 128), F32),
                vmem((T, 2 * DV), BF16),
                vmem((T, 2 * DV), BF16),
                vmem((2, T, COLS), F32),
                vmem((PIECES, ROWS, COLS), BF16),
                vmem((PIECES, ROWS, COLS), BF16),
                vmem((2, 2 * DV, COLS), BF16),
                vmem((T, COLS), BF16),
                dma((9,)),
                dma((2,)),
                dma((2,)),
                dma((2, nz)),
                dma((2, nx)),
                dma((2,)),
                dma((2, nz)),
                dma((2, nx)),
                dma((2, nz)),
                dma((2, nz)),
                dma((2, 2)),
                dma((2, 2, 2)),
                dma((2, 2, 2)),
                dma((2, 2, nx)),
                dma((2, PIECES)),
                dma((2, PIECES)),
                dma((PIECES,)),
            ],
            compiler_params=pltpu.CompilerParams(
                collective_id=0, has_side_effects=True, vmem_limit_bytes=56 * 1024 * 1024
            ),
        )(
            conv_in, conv_weight, conv_bias.reshape(1, -1), qk_weight, value_in, gate_pre,
            norm_gain.reshape(1, -1), out_weight,
        )

    return jax.shard_map(
        body,
        mesh=mesh,
        in_specs=(
            P("ctx", "head"),
            P(None, "head"),
            P("head"),
            P(None, "head", None, None),
            P("ctx", "head"),
            P(None, "head", "ctx"),
            P("head"),
            P("head", None),
        ),
        out_specs=P("ctx", "head"),
        check_vma=False,
    )
```

time: 84.4 us -> 73 us (0.86)
  Pallas kernels: 82 us -> 70.6 us
    pallas_call x1, Pallas kernels: 82 us -> 70.6 us  [body(): pl.pallas_call(body_kernel, out_shape=jax.ShapeDtypeStruct((T, COLS), BF1...]
where the time goes in v2:
time: 73 us; the launch traced here: 72.9 us
  Pallas kernels  70.6 us (97%)
  local copies, waits for them, and re-layouts  2.26 us (3%)
    pallas_call x1, Pallas kernels, body(): pl.pallas_call(body_kernel, out_shape=jax.ShapeDtypeStruct((T, COLS), BF1...  70.6 us
    unnamed x1, local copies, waits for them, and re-layouts  2.26 us

profile of v2, /device:TPU:1, one launch (start us, length us, event | category | flops | bytes accessed | tf_op | source)
XLA Modules:
  0.0 72.9 jit_solution(14290070700481908736)
XLA Ops:
  0.0 70.6 %shard_map.82 = bf16[512,1024]{1,0:T(8,128)(2,1)} custom-call(bf16[512,512]{1,0:T(8,128)(2,1)} %conv_hbm.1, f32[4,512]{1,0:T(4,128)} %cw_hbm.1, f32[1,512]{1,0:T(1,128)} %bitcast.3, bf16[2,2,256,256]{3,2,1,0:T(8,128)(2,1)} %qk_hbm.1, bf16[512,1024]{1,0:T(8,128)(2,1)} %val_hbm.1, f32[2,2,512]{2,1,0:T(2,128)} %gate_hbm.1, f32[1,1024]{1,0:T(1,128)} %bitcast.2, ...), custom_call_target="tpu_custom_call" | custom-call | tf_op jit(solution)/shard_map/pallas_call | solution.py:515
  70.6 2.3 %copy.10 = bf16[512,1024]{1,0:T(8,128)(2,1)} copy(bf16[512,1024]{1,0:T(8,128)(2,1)} %shard_map.82) | data formatting | bytes 2097152

commit v3 on v2

--- a/solution.py
+++ b/solution.py
@@ -21,8 +21,9 @@
 ROWS = 64
 PIECES = T // ROWS
 LATE = 128
-AHEAD = 2
-LAG = 2
+EDGE = 16
+SMALL = 16
+LAG = 3
 
 
 def dot(a, b):
@@ -45,12 +46,12 @@
 
 def body_kernel(
     conv_hbm, cw_hbm, cb_hbm, qk_hbm, val_hbm, gate_hbm, gain_hbm, w_hbm,
-    out_hbm,
+    out,
     conv_v, cw, cb, qk, val, gate, gain, w, xpad, halo, act, q, kt, state, state_oth, local,
     sc_own, sc_other, sc_chip, sc_row, st_send, st_recv, t_send, t_in, r_send, r_in,
-    c_send, c_factor, c_in, p_send, carry, cm_col, normed, normed_in, acc, part_s, part_r, w_far, out_v,
+    c_send, c_factor, c_in, p_send, carry, cm_col, normed, normed_in, acc, part_s, part_r, w_far,
     ld_sem, halo_sem, sc_sem, scz_sem, scx_sem, st_sem, tz_sem, rx_sem, cz_sem, p_sem,
-    wy_sem, wx_sem, wh_sem, wc_sem, ag_sem, rs_sem, out_sem,
+    wy_sem, wx_sem, wh_sem, wc_sem, ag_sem, rs_sem,
 ):
     nx, nz = NX, NZ
     n_ctx = nx * nz * 2
@@ -191,16 +192,19 @@
 
     lax.fori_loop(0, T // rows, widen, 0)
 
-    def conv(i, _):
-        r = pl.multiple_of(i * rows, rows)
-        ext = xpad[pl.ds(r, rows + 8), :]
-        pre = cb[0:1, :] + cw[0:1, :] * ext[5 : 5 + rows]
+    def conv(r, n):
+        ext = xpad[pl.ds(r, n + 8), :]
+        pre = cb[0:1, :] + cw[0:1, :] * ext[5 : 5 + n]
         for j in range(1, 4):
-            pre = pre + cw[j : j + 1, :] * ext[5 + j : 5 + j + rows]
-        act[pl.ds(r, rows), :] = (pre / (1.0 + jnp.exp(-pre))).astype(BF16)
+            pre = pre + cw[j : j + 1, :] * ext[5 + j : 5 + j + n]
+        act[pl.ds(r, n), :] = (pre / (1.0 + jnp.exp(-pre))).astype(BF16)
+
+    def conv_step(i, _):
+        conv(pl.multiple_of(i * rows, rows), rows)
         return 0
 
-    lax.fori_loop(LATE // rows, T // rows, conv, 0)
+    conv(EDGE, rows - EDGE)
+    lax.fori_loop(1, T // rows, conv_step, 0)
 
     loads[4].wait()
     loads[5].wait()
@@ -230,7 +234,7 @@
     halo_copy.wait()
     edge = halo[...].astype(F32)[8:16]
     xpad[0:8, :] = jnp.where(me > 0, edge, 0.0)
-    lax.fori_loop(0, LATE // rows, conv, 0)
+    conv(0, EDGE)
     project(1 - core, 0, LATE)
     st_send[...] = (state_oth[...] + block_state(1 - core, scale_oth, 0, LATE)).astype(BF16)
     st_copy = remote(st_send, st_recv, (st_sem.at[0], st_sem.at[1]), other)
@@ -329,7 +333,6 @@
         copy.start()
         rx.append(copy)
     r_in[x] = r_send[...]
-    w_first(1)
     run = t_in[0].astype(F32) * add[0]
     c_send[1] = run
     for k in range(1, nz - 1):
@@ -384,6 +387,7 @@
         cz[k] = copy
     c_in[z] = carried(z)
     w_second(0)
+    w_first(1)
 
     def p_copy(k):
         at = slice_of(lax.rem(z + nz - k, nz))
@@ -410,97 +414,128 @@
     loads[6].wait()
     loads[7].wait()
     loads[8].wait()
+
+    def token(i):
+        return pl.ds(pl.multiple_of(i * ROWS, ROWS), ROWS)
+
+    def norm(i, h):
+        at = token(i)
+        col = pl.ds(pl.multiple_of(h * DV, DV), DV)
+        column = cm_col[at, :]
+        gap = jnp.where(h == 0, carry_m[0:1, 0:1] - column[:, 0:1], carry_m[1:2, 0:1] - column[:, 1:2])
+        top = jnp.maximum(gap, 0.0)
+        total = local[h, at, :] * jnp.exp(-top) + jnp.exp(gap - top) * dot(q[h, at, :], carry[h])
+        scale = lax.rsqrt(jnp.mean(total * total, axis=1, keepdims=True) + 1e-6)
+        normed[at, col] = (total * scale * gain[0:1, col]).astype(BF16)
+
+    def each(lo, hi, fn):
+        def step(i, _):
+            fn(i)
+            return 0
+
+        lax.fori_loop(lo, hi, step, 0)
+
+    LAST = PIECES - 1
+    first_a = (LAST + 1, pl.ds(0, SMALL))
+    first_b = (0, pl.ds(SMALL, ROWS - SMALL))
+    last_a = (LAST, pl.ds(LAST * ROWS, ROWS - SMALL))
+    last_b = (LAST + 2, pl.ds(T - SMALL, SMALL))
+
+    def ag_copy(slot, at):
+        return remote(normed.at[at], normed_in.at[at], (ag_sem.at[0, slot], ag_sem.at[1, slot]), me, pair)
+
+    def rs_copy(slot, at):
+        return remote(part_s.at[at], part_r.at[at], (rs_sem.at[0, slot], rs_sem.at[1, slot]), me, mate)
+
+    def own(side, lo, hi):
+        def step(i):
+            at = pl.ds(pl.multiple_of(i * 256, 256), 256)
+            acc[side, lo:hi, at] = dot(normed[lo:hi, :], w[side, :, at])
+
+        each(0, COLS // 256, step)
+
+    def work(slot, at):
+        ag_copy(slot, at).wait_recv()
+        part_s[at, :] = (acc[0, at, :] + dot(normed_in[at, :], w_far[0])).astype(BF16)
+        rs_copy(slot, at).start()
+
+    def here(i):
+        acc[1, token(i), :] = acc[1, token(i), :] + dot(normed_in[token(i), :], w_far[1])
+
+    def add(i):
+        out[token(i), :] = (acc[1, token(i), :] + part_r[token(i), :].astype(F32)).astype(BF16)
+
+    each(0, PIECES, lambda i: norm(i, core))
     w_third(0)
     for k in range(nz):
         p_copy(k).wait_send()
         p_arrival(k).wait_recv()
-
-    def token(i):
-        return pl.ds(pl.multiple_of(i * ROWS, ROWS), ROWS)
-
-    def norm(i):
-        at = token(i)
-        column = cm_col[at, :]
-        for h in range(2):
-            gap = carry_m[h : h + 1, 0:1] - column[:, h : h + 1]
-            top = jnp.maximum(gap, 0.0)
-            total = local[h, at, :] * jnp.exp(-top) + jnp.exp(gap - top) * dot(q[h, at, :], carry[h])
-            scale = lax.rsqrt(jnp.mean(total * total, axis=1, keepdims=True) + 1e-6)
-            normed[at, h * DV : (h + 1) * DV] = (
-                total * scale * gain[0:1, h * DV : (h + 1) * DV]
-            ).astype(BF16)
-
-    def ag_copy(i):
-        return remote(normed.at[token(i)], normed_in.at[token(i)], (ag_sem.at[0, i], ag_sem.at[1, i]), me, pair)
-
-    def rs_copy(i):
-        return remote(part_s.at[i], part_r.at[i], (rs_sem.at[0, i], rs_sem.at[1, i]), me, mate)
-
-    def out_copy(i):
-        return pltpu.make_async_copy(out_v.at[token(i)], out_hbm.at[token(i)], out_sem.at[i])
-
-    def each(lo, hi, fn):
-        def step(i, _):
-            fn(i)
-            return 0
-
-        lax.fori_loop(lo, hi, step, 0)
-
-    def norm_and_send(i):
-        norm(i)
-        ag_copy(i).start()
-
-    each(0, AHEAD, norm_and_send)
-    each(AHEAD, PIECES, norm)
-
-    def own(i):
-        at = pl.ds(pl.multiple_of(lax.rem(i, 4) * 256, 256), 256)
-        acc[lax.div(i, 4), :, at] = dot(normed[...], w[lax.div(i, 4), :, at])
-
-    each(0, 8, own)
+    norm(0, 1 - core)
+    ag_copy(*first_a).start()
+    ag_copy(*first_b).start()
+    norm(1, 1 - core)
+    ag_copy(1, token(1)).start()
+    norm(2, 1 - core)
+    ag_copy(2, token(2)).start()
+    own(0, 0, ROWS)
+    w_wait(0)
+    work(*first_a)
+    each(3, PIECES, lambda i: norm(i, 1 - core))
+    work(*first_b)
+    own(0, ROWS, T)
     w_second(1)
-    w_wait(0)
-
-    def finish(i):
-        rs_copy(i).wait_recv()
-        total = acc[1, token(i), :] + part_r[i].astype(F32)
-        out_v[token(i), :] = total.astype(BF16)
-        out_copy(i).start()
-
-    def work(i):
-        ag_copy(i).wait_recv()
-
-        @pl.when(i + AHEAD < PIECES)
+    own(1, 0, T)
+
+    def middle(i):
+        ag_copy(i, token(i)).wait_send()
+
+        @pl.when(i + 2 < LAST)
         def _():
-            ag_copy(i).wait_send()
-            ag_copy(i + AHEAD).start()
-
-        far = normed_in[token(i), :]
-        part_s[i] = (acc[0, token(i), :] + dot(far, w_far[0])).astype(BF16)
-        rs_copy(i).start()
-
-    each(0, LAG, work)
-
-    def here(i):
-        acc[1, token(i), :] = acc[1, token(i), :] + dot(normed_in[token(i), :], w_far[1])
-
-    def both(i):
-        work(i)
-        here(i - LAG)
-        finish(i - LAG)
-
+            ag_copy(i + 2, token(i + 2)).start()
+
+        @pl.when(i + 2 == LAST)
+        def _():
+            ag_copy(*last_a).start()
+
+        @pl.when(i + 2 == LAST + 1)
+        def _():
+            ag_copy(*last_b).start()
+
+        work(i, token(i))
+
+    each(1, LAG, middle)
     w_third(1)
     w_wait(1)
-    each(LAG, PIECES, both)
-    each(PIECES - LAG, PIECES, here)
-    each(PIECES - LAG, PIECES, finish)
-
-    def drain(i):
-        rs_copy(i).wait_send()
-        out_copy(i).wait()
-
-    each(0, PIECES, drain)
-    each(PIECES - AHEAD, PIECES, lambda i: ag_copy(i).wait_send())
+    each(0, LAG - 1, here)
+    rs_copy(*first_a).wait_recv()
+    rs_copy(*first_b).wait_recv()
+    add(0)
+
+    def both(i):
+        middle(i)
+        here(i - 1)
+
+        @pl.when(i > LAG)
+        def _():
+            rs_copy(i - LAG, token(i - LAG)).wait_recv()
+            add(i - LAG)
+
+    each(LAG, LAST, both)
+    work(*last_a)
+    here(LAST - 1)
+    work(*last_b)
+    here(LAST)
+    for i in range(LAST - LAG, LAST):
+        rs_copy(i, token(i)).wait_recv()
+        add(i)
+    rs_copy(*last_a).wait_recv()
+    rs_copy(*last_b).wait_recv()
+    add(LAST)
+
+    for piece in (first_a, first_b, last_a, last_b):
+        ag_copy(*piece).wait_send()
+        rs_copy(*piece).wait_send()
+    each(1, LAST, lambda i: rs_copy(i, token(i)).wait_send())
     w_drain(0)
     w_drain(1)
 
@@ -514,9 +549,9 @@
         vmem = pltpu.VMEM
         return pl.pallas_call(
             body_kernel,
-            out_shape=jax.ShapeDtypeStruct((T, COLS), BF16),
+            out_shape=vmem((T, COLS), BF16),
             in_specs=[pl.BlockSpec(memory_space=pl.ANY)] * 8,
-            out_specs=pl.BlockSpec(memory_space=pl.ANY),
+            out_specs=pl.BlockSpec(memory_space=vmem),
             scratch_shapes=[
                 vmem((T, 2 * DK), BF16),
                 vmem((4, 2 * DK), F32),
@@ -553,10 +588,9 @@
                 vmem((T, 2 * DV), BF16),
                 vmem((T, 2 * DV), BF16),
                 vmem((2, T, COLS), F32),
-                vmem((PIECES, ROWS, COLS), BF16),
-                vmem((PIECES, ROWS, COLS), BF16),
+                vmem((T, COLS), BF16),
+                vmem((T, COLS), BF16),
                 vmem((2, 2 * DV, COLS), BF16),
-                vmem((T, COLS), BF16),
                 dma((9,)),
                 dma((2,)),
                 dma((2,)),
@@ -571,9 +605,8 @@
                 dma((2, 2, 2)),
                 dma((2, 2, 2)),
                 dma((2, 2, nx)),
-                dma((2, PIECES)),
-                dma((2, PIECES)),
-                dma((PIECES,)),
+                dma((2, PIECES + 2)),
+                dma((2, PIECES + 2)),
             ],
             compiler_params=pltpu.CompilerParams(
                 collective_id=0, has_side_effects=True, vmem_limit_bytes=56 * 1024 * 1024

time: 73 us -> 70.6 us (0.967)
  local copies, waits for them, and re-layouts: 2.26 us -> 0.97 us
  Pallas kernels: 70.6 us -> 69.4 us
    unnamed x1, local copies, waits for them, and re-layouts: 2.26 us -> 0.97 us
    pallas_call x1, Pallas kernels: 70.6 us -> 69.4 us  [body(): pl.pallas_call(body_kernel, out_shape=vmem((T, COLS), BF16), in_specs=[pl...]
where the time goes in v3:
time: 70.6 us; the launch traced here: 70.4 us
  Pallas kernels  69.4 us (98%)
  local copies, waits for them, and re-layouts  0.97 us (1%)
    pallas_call x1, Pallas kernels, body(): pl.pallas_call(body_kernel, out_shape=vmem((T, COLS), BF16), in_specs=[pl...  69.4 us

profile of v3, /device:TPU:1, one launch (start us, length us, event | category | flops | bytes accessed | tf_op | source)
XLA Modules:
  0.0 70.4 jit_solution(4803933861330544294)
XLA Ops:
  0.0 69.4 %shard_map.82 = bf16[512,1024]{1,0:T(8,128)(2,1)S(1)} custom-call(bf16[512,512]{1,0:T(8,128)(2,1)} %conv_hbm.1, f32[4,512]{1,0:T(4,128)} %cw_hbm.1, f32[1,512]{1,0:T(1,128)} %bitcast.3, bf16[2,2,256,256]{3,2,1,0:T(8,128)(2,1)} %qk_hbm.1, bf16[512,1024]{1,0:T(8,128)(2,1)} %val_hbm.1, f32[2,2,512]{2,1,0:T(2,128)} %gate_hbm.1, f32[1,1024]{1,0:T(1,128)} %bitcast.2, ...), custom_call_target="tpu_custom_call" | custom-call | tf_op jit(solution)/shard_map/pallas_call | solution.py:550
  69.4 1.0 %copy.10 = bf16[512,1024]{1,0:T(8,128)(2,1)} copy(bf16[512,1024]{1,0:T(8,128)(2,1)S(1)} %shard_map.82) | data formatting | bytes 2097152

commit v4 on v3

--- a/solution.py
+++ b/solution.py
@@ -88,9 +88,6 @@
              (w_hbm.at[:, pl.ds(pl.multiple_of(y * COLS, COLS), COLS)], w.at[1])]
         )
     ]
-    for load in loads:
-        load.start()
-
     barrier = pltpu.get_barrier_semaphore()
     after = lax.rem(me + 1, n_ctx)
     before = lax.rem(me + n_ctx - 1, n_ctx)
@@ -100,6 +97,8 @@
     greet += [(me, pair), (me, mate)]
     for to in greet:
         pl.semaphore_signal(barrier, inc=1, device_id=to, device_id_type=MESH)
+    for load in loads:
+        load.start()
 
     loads[0].wait()
     pad = jnp.zeros((6, T), F32)
@@ -131,19 +130,20 @@
         row = pl.multiple_of((lax.rem(at_x + nx, nx) * 2 + core) * w_rows + lo, 16)
         return w_far.at[j, pl.ds(row, count), :]
 
+    def y_copy(j, at_x, sems):
+        column = pl.multiple_of((NY - 1 - pair if j == 0 else pair) * COLS, COLS)
+        row = pl.multiple_of((lax.rem(at_x, nx) * 2 + core) * w_rows, w_rows)
+        return remote(w_hbm.at[pl.ds(row, w_rows), pl.ds(column, COLS)], w_piece(j, at_x), sems, me, pair)
+
     def wy_copy(j):
-        column = pl.multiple_of((NY - 1 - pair if j == 0 else pair) * COLS, COLS)
-        row = pl.multiple_of((x * 2 + core) * w_rows, w_rows)
-        return remote(w_hbm.at[pl.ds(row, w_rows), pl.ds(column, COLS)], w_piece(j, x),
-                      (wy_sem.at[0, j], wy_sem.at[1, j]), me, pair)
+        return y_copy(j, x, (wy_sem.at[0, j], wy_sem.at[1, j]))
+
+    def wh_copy(j):
+        return y_copy(j, x + 2, (wh_sem.at[0, j], wh_sem.at[1, j]))
 
     def wx_copy(j, side):
         piece = w_piece(j, x)
         return remote(piece, piece, (wx_sem.at[0, j, side], wx_sem.at[1, j, side]), x_peer((1, nx - 1)[side]))
-
-    def wh_copy(j, side):
-        piece = w_piece(j, x + (-1, 1)[side], side * (w_rows // 2), w_rows // 2)
-        return remote(piece, piece, (wh_sem.at[0, j, side], wh_sem.at[1, j, side]), x_peer((1, nx - 1)[side]))
 
     def wc_copy(j, k):
         piece = w_piece(j, x + k)
@@ -154,18 +154,14 @@
         wx_copy(j, 0).start()
         wx_copy(j, 1).start()
         wc_copy(j, 0).start()
-        if j == 0:
-            wy_copy(1).start()
 
     def w_second(j):
         for side in range(2):
             wx_copy(j, side).wait_recv()
-            wh_copy(j, side).start()
             wc_copy(j, (nx - 1, 1)[side]).start()
 
     def w_third(j):
-        for side in range(2):
-            wh_copy(j, side).wait_recv()
+        wh_copy(j).wait_recv()
         wc_copy(j, 2).start()
 
     def w_wait(j):
@@ -174,9 +170,9 @@
 
     def w_drain(j):
         wy_copy(j).wait_send()
+        wh_copy(j).wait_send()
         for side in range(2):
             wx_copy(j, side).wait_send()
-            wh_copy(j, side).wait_send()
 
     wy_copy(0).start()
 
@@ -239,6 +235,7 @@
     st_send[...] = (state_oth[...] + block_state(1 - core, scale_oth, 0, LATE)).astype(BF16)
     st_copy = remote(st_send, st_recv, (st_sem.at[0], st_sem.at[1]), other)
     st_copy.start()
+    wh_copy(0).start()
     project(core, 0, LATE)
     state[...] = state[...] + block_state(core, scale_own, 0, LATE)
 
@@ -311,6 +308,7 @@
 
     inner(0)
     inner(1)
+    wy_copy(1).start()
 
     to_row = []
     m, d = jnp.full((8, 128), LOW, F32), jnp.zeros((8, 128), F32)
@@ -387,7 +385,9 @@
         cz[k] = copy
     c_in[z] = carried(z)
     w_second(0)
+    w_third(0)
     w_first(1)
+    wh_copy(1).start()
 
     def p_copy(k):
         at = slice_of(lax.rem(z + nz - k, nz))
@@ -466,7 +466,6 @@
         out[token(i), :] = (acc[1, token(i), :] + part_r[token(i), :].astype(F32)).astype(BF16)
 
     each(0, PIECES, lambda i: norm(i, core))
-    w_third(0)
     for k in range(nz):
         p_copy(k).wait_send()
         p_arrival(k).wait_recv()
@@ -478,9 +477,9 @@
     norm(2, 1 - core)
     ag_copy(2, token(2)).start()
     own(0, 0, ROWS)
+    each(3, PIECES, lambda i: norm(i, 1 - core))
     w_wait(0)
     work(*first_a)
-    each(3, PIECES, lambda i: norm(i, 1 - core))
     work(*first_b)
     own(0, ROWS, T)
     w_second(1)
@@ -603,7 +602,7 @@
                 dma((2, nz)),
                 dma((2, 2)),
                 dma((2, 2, 2)),
-                dma((2, 2, 2)),
+                dma((2, 2)),
                 dma((2, 2, nx)),
                 dma((2, PIECES + 2)),
                 dma((2, PIECES + 2)),

time: 70.6 us -> 69.8 us (0.989)
    pallas_call x1, Pallas kernels: 69.4 us -> 68.7 us  [body(): pl.pallas_call(body_kernel, out_shape=vmem((T, COLS), BF16), in_specs=[pl...]
where the time goes in v4:
time: 69.8 us; the launch traced here: 69.7 us
  Pallas kernels  68.7 us (98%)
  local copies, waits for them, and re-layouts  0.97 us (1%)
    pallas_call x1, Pallas kernels, body(): pl.pallas_call(body_kernel, out_shape=vmem((T, COLS), BF16), in_specs=[pl...  68.7 us

profile of v4, /device:TPU:1, one launch (start us, length us, event | category | flops | bytes accessed | tf_op | source)
XLA Modules:
  0.0 69.7 jit_solution(11696008756826198145)
XLA Ops:
  0.0 68.7 %shard_map.82 = bf16[512,1024]{1,0:T(8,128)(2,1)S(1)} custom-call(bf16[512,512]{1,0:T(8,128)(2,1)} %conv_hbm.1, f32[4,512]{1,0:T(4,128)} %cw_hbm.1, f32[1,512]{1,0:T(1,128)} %bitcast.3, bf16[2,2,256,256]{3,2,1,0:T(8,128)(2,1)} %qk_hbm.1, bf16[512,1024]{1,0:T(8,128)(2,1)} %val_hbm.1, f32[2,2,512]{2,1,0:T(2,128)} %gate_hbm.1, f32[1,1024]{1,0:T(1,128)} %bitcast.2, ...), custom_call_target="tpu_custom_call" | custom-call | tf_op jit(solution)/shard_map/pallas_call | solution.py:549
  68.7 1.0 %copy.10 = bf16[512,1024]{1,0:T(8,128)(2,1)} copy(bf16[512,1024]{1,0:T(8,128)(2,1)S(1)} %shard_map.82) | data formatting | bytes 2097152

commit v5 on v4

--- a/solution.py
+++ b/solution.py
@@ -91,8 +91,8 @@
     barrier = pltpu.get_barrier_semaphore()
     after = lax.rem(me + 1, n_ctx)
     before = lax.rem(me + n_ctx - 1, n_ctx)
-    greet = [(after, y), (before, y), (other, y)]
-    greet += [(z_peer(k), y) for k in range(1, nz)]
+    greet = [(z_peer(k), y) for k in FAR_FIRST]
+    greet += [(after, y), (before, y), (other, y)]
     greet += [(x_peer(k), y) for k in range(1, nx)]
     greet += [(me, pair), (me, mate)]
     for to in greet:
@@ -483,7 +483,6 @@
     work(*first_b)
     own(0, ROWS, T)
     w_second(1)
-    own(1, 0, T)
 
     def middle(i):
         ag_copy(i, token(i)).wait_send()
@@ -502,7 +501,10 @@
 
         work(i, token(i))
 
-    each(1, LAG, middle)
+    middle(1)
+    own(1, 0, HALF)
+    each(2, LAG, middle)
+    own(1, HALF, T)
     w_third(1)
     w_wait(1)
     each(0, LAG - 1, here)

time: 69.8 us -> 71.4 us (1.023)
  Pallas kernels: 68.7 us -> 70.3 us
    pallas_call x1, Pallas kernels: 68.7 us -> 70.3 us  [body(): pl.pallas_call(body_kernel, out_shape=vmem((T, COLS), BF16), in_specs=[pl...]
where the time goes in v5:
time: 71.4 us; the launch traced here: 71.3 us
  Pallas kernels  70.3 us (98%)
  local copies, waits for them, and re-layouts  0.97 us (1%)
    pallas_call x1, Pallas kernels, body(): pl.pallas_call(body_kernel, out_shape=vmem((T, COLS), BF16), in_specs=[pl...  70.3 us

profile of v5, /device:TPU:1, one launch (start us, length us, event | category | flops | bytes accessed | tf_op | source)
XLA Modules:
  0.0 71.3 jit_solution(16786556444743299837)
XLA Ops:
  0.0 70.3 %shard_map.82 = bf16[512,1024]{1,0:T(8,128)(2,1)S(1)} custom-call(bf16[512,512]{1,0:T(8,128)(2,1)} %conv_hbm.1, f32[4,512]{1,0:T(4,128)} %cw_hbm.1, f32[1,512]{1,0:T(1,128)} %bitcast.3, bf16[2,2,256,256]{3,2,1,0:T(8,128)(2,1)} %qk_hbm.1, bf16[512,1024]{1,0:T(8,128)(2,1)} %val_hbm.1, f32[2,2,512]{2,1,0:T(2,128)} %gate_hbm.1, f32[1,1024]{1,0:T(1,128)} %bitcast.2, ...), custom_call_target="tpu_custom_call" | custom-call | tf_op jit(solution)/shard_map/pallas_call | solution.py:551
  70.3 1.0 %copy.10 = bf16[512,1024]{1,0:T(8,128)(2,1)} copy(bf16[512,1024]{1,0:T(8,128)(2,1)S(1)} %shard_map.82) | data formatting | bytes 2097152
